TPU v7x, 256 devices: a whole 4x4x8 slice. The times are simulated.
256 devices in a mesh: row: 16 (over x_hi, z), col: 4 (over y), depth: 4 (over x_lo, core).
Axes of the slice: x: 4 (x_hi: 2, x_lo: 2; x = x_hi * 2 + x_lo), y: 4, z: 8, core: 2. Of those that a mesh axis runs over, the one named last changes fastest.
Arguments:
- basis: bfloat16 [4, 512, 65536], P('depth', 'row', 'col'), may hold values from -0.1875 to 0.1875
- targets: bfloat16 [4, 512, 4096], P('depth', 'col', 'row'), may hold values from -6 to 6
Outputs:
- cross: float32 [65536, 4096], P(('col', 'depth'), 'row')
All inputs are finite; a program needn't handle non-finite values.
Results may differ from a plain program's by a relative error of at most 0.0003.
Values may be sent and summed in bfloat16 or wider, within the bound.
A program may use at most 128 MiB of HBM per device.

v0:
```python
import jax
import jax.numpy as jnp
from jax import lax
from jax.sharding import PartitionSpec as P


def per_device(basis, targets):
    layer_targets = lax.all_gather(targets, "col", axis=1, tiled=True)
    matched = layer_targets[0]
    partial_cross = jnp.einsum(
        "sk,so->ko",
        lax.all_gather(basis, "row", axis=1, tiled=True)[0],
        matched,
        preferred_element_type=jnp.float32,
    )
    return lax.psum_scatter(partial_cross, "depth", scatter_dimension=0, tiled=True)


def solution(mesh):
    in_specs = (P("depth", "row", "col"), P("depth", "col", "row"))
    out_specs = P(("col", "depth"), "row")
    return jax.shard_map(
        per_device, mesh=mesh, in_specs=in_specs, out_specs=out_specs, check_vma=False
    )
```

profile of v0, /device:TPU:1, one launch (start us, length us, event | category | flops | bytes accessed | tf_op | source)
XLA Modules:
  0.0 408.0 jit_solution(12334591027573544213)
XLA Ops:
  6.5 0.0 all-gather.2.cloned.1.call-start
  6.5 0.7 all-gather.2.cloned.1.call-update
  7.3 0.0 reduce-scatter.2.cloned.1.call-start
  7.3 11.5 %all_gather.7 = bf16[1,512,256]{2,1,0:T(8,128)(2,1)S(1)} all-gather(bf16[1,128,256]{2,1,0:T(8,128)(2,1)} %param.3), channel_id=1, replica_groups=mesh['row'=16,'col'=4,'depth'=4] {'col'}, dimensions={1}, use_global_device_ids=true | all-gather | bytes 327680 | tf_op jit(solution)/shard_map/all_gather | solution.py:8
  18.8 219.6 %all-gather.2.cloned.1.call-done = bf16[1,512,16384]{2,1,0:T(8,128)(2,1)} async-done(((bf16[1,32,16384]{2,1,0:T(8,128)(2,1)}), bf16[1,512,16384]{2,1,0:T(8,128)(2,1)}) %all-gather.2.cloned.1.call-update) | async-done | bytes 16777232 | tf_op jit(solution)/shard_map/all_gather | solution.py:12
  238.4 16.0 %fusion = f32[16384,256]{1,0:T(8,128)} fusion(bf16[1,512,16384]{2,1,0:T(8,128)(2,1)} %all-gather.2.cloned.1.call-done, bf16[1,512,256]{2,1,0:T(8,128)(2,1)S(1)} %all_gather.7), kind=kOutput, calls=%fused_computation | convolution fusion | flops 4294967296 | bytes 33816576 | tf_op jit(solution)/shard_map/sk,so->ko/dot_general | solution.py:10
  254.4 0.0 reduce-scatter.2.cloned.1.call-update
  254.5 146.7 %reduce-scatter.2.cloned.1.call-done = f32[4096,256]{1,0:T(8,128)} async-done(((f32[16384,256]{1,0:T(8,128)}), f32[4096,256]{1,0:T(8,128)}) %reduce-scatter.2.cloned.1.call-update) | async-done | bytes 4194320 | tf_op jit(solution)/shard_map/reduce_scatter | solution.py:16
Async XLA Ops:
  6.5 231.9 %all-gather.2.cloned.1.call-start = ((), (), s32[]{:S(2)}) async-start(), calls=%async_computation.1 | async-start | bytes 17825792 | tf_op jit(solution)/shard_map/all_gather | solution.py:12
  7.3 393.9 %reduce-scatter.2.cloned.1.call-start = ((), (), s32[]{:S(2)}) async-start(), calls=%async_computation.2 | async-start | bytes 20971520 | tf_op jit(solution)/shard_map/reduce_scatter | solution.py:16
Sparse Core Ops, SparseCore 0:
  9.9 228.4 all-gather.1
  254.6 146.5 reduce-scatter.1
where the time goes:
time: 408 us
  waiting for transfers between devices  367 us (90%)
  matrix products  16 us (4%)
  between operations  13.4 us (3%)
  blocking collectives  11.5 us (3%)
    all_gather x1, waiting for transfers between devices, per_device(): lax.all_gather(basis, 'row', axis=1, tiled=True)[0]  220 us
    reduce_scatter x1, waiting for transfers between devices, per_device(): lax.psum_scatter(partial_cross, 'depth', scatter_dimension=0, tiled=True)  147 us
    dot_general x1, matrix products, per_device(): jnp.einsum('sk,so->ko', lax.all_gather(basis, 'row', axis=1, tiled=True)[...  16 us
    all_gather x1, blocking collectives, per_device(): layer_targets = lax.all_gather(targets, 'col', axis=1, tiled=True)  11.5 us
  transfers between devices with their start and end apart: 2, of which 2 were waited for; matrix products, arithmetic and copies ran while one was open for 0% of the time, Pallas kernels for 0%

commit v1 on v0

v1 whole, which is shorter than its diff:
```python
import jax
import jax.numpy as jnp
from jax import lax
from jax.experimental import pallas as pl
from jax.experimental.pallas import tpu as pltpu
from jax.sharding import PartitionSpec as P

MESH = pl.DeviceIdType.MESH
NZ = 8
NX = 8
CHUNKS = 8
GROUP = 2


def kernel(
    basis, targets, out, gath, tg, ob,
    x_send, x_recv, z_send, z_recv, t_send, t_recv, o_send, o_recv,
):
    tile = gath.shape[0] * gath.shape[2]
    kc = gath.shape[2]
    rows = basis.shape[0]
    piece = NX * rows
    half = piece // 2
    row, y, d = (lax.axis_index(a) for a in ("row", "col", "depth"))
    hi, z = row // NZ, row % NZ
    me = hi * 4 + d
    up, down = (z + 1) % NZ, (z + NZ - 1) % NZ

    def x_peer(idx):
        return ((idx // 4) * NZ + z, y, idx % 4)

    def z_peer(zz):
        return (hi * NZ + zz, y, d)

    def y_peer(yy):
        return (row, yy, d)

    barrier = pltpu.get_barrier_semaphore()
    for i in range(1, NX):
        pl.semaphore_signal(barrier, inc=1, device_id=x_peer((me + i) % NX), device_id_type=MESH)
    for zz in (up, down):
        pl.semaphore_signal(barrier, inc=1, device_id=z_peer(zz), device_id_type=MESH)
    for i in range(1, 4):
        pl.semaphore_signal(barrier, inc=1, device_id=y_peer((y + i) % 4), device_id_type=MESH)
    pl.semaphore_wait(barrier, NX - 1 + 2 + 3)

    def columns(idx, c):
        owner = (1 - (idx % 4) // 2) * 2 + idx % 2
        start = owner * 2 * tile + (idx // 4) * tile + c * kc
        return pl.ds(pl.multiple_of(start, kc), kc)

    def scatter_basis(c):
        mine = gath.at[c, pl.ds(pl.multiple_of(z * piece + me * rows, rows), rows), :]
        for i in range(1, NX):
            idx = (me + i) % NX
            pltpu.make_async_remote_copy(
                basis.at[:, columns(idx, c)], mine, x_send, x_recv.at[c],
                device_id=x_peer(idx), device_id_type=MESH,
            ).start()
        pltpu.make_async_copy(basis.at[:, columns(me, c)], mine, x_recv.at[c]).start()

    def origin(c, zz, first=0, count=piece):
        return gath.at[c, pl.ds(pl.multiple_of(zz * piece + first, half), count), :]

    def wait_bytes(ref, sem):
        pltpu.make_async_copy(ref, ref, sem).wait()

    def part(way, hop):
        if hop < 3:
            return 0, piece
        return (0, half) if way == 0 else (half, half)

    def z_origin(way, hop):
        return (z - hop + NZ) % NZ if way == 0 else (z + hop) % NZ

    def z_copy(c, way, hop):
        ref = origin(c, z_origin(way, hop), *part(way, hop))
        return pltpu.make_async_remote_copy(
            ref, ref, z_send.at[way], z_recv.at[way, c, hop],
            device_id=z_peer(up if way == 0 else down), device_id_type=MESH,
        )

    def z_wait(c, way, hop):
        ref = origin(c, z_origin(way, hop + 1), *part(way, hop))
        wait_bytes(ref, z_recv.at[way, c, hop])

    def t_region(yy):
        return tg.at[:, pl.ds((yy % 2) * 4, 4), pl.ds((yy // 2) * 4, 4), :, :]

    def t_own():
        return tg.at[hi, pl.ds((y % 2) * 4, 4), (y // 2) * 4 + d, :, :]

    def gather_targets_x():
        for i in range(1, NX):
            pltpu.make_async_remote_copy(
                targets, t_own(), t_send.at[0], t_recv.at[0],
                device_id=x_peer((me + i) % NX), device_id_type=MESH,
            ).start()
        pltpu.make_async_copy(targets, t_own(), t_recv.at[0]).start()

    def gather_targets_y():
        wait_bytes(t_region(y), t_recv.at[0])
        for i in (2, 1, 3):
            pltpu.make_async_remote_copy(
                t_region(y), t_region(y), t_send.at[1], t_recv.at[1],
                device_id=y_peer((y + i) % 4), device_id_type=MESH,
            ).start()

    def multiply(c):
        a = gath[c]
        for h in range(2):
            ob[c, h] = lax.dot_general(
                a, tg[h].reshape(NZ * piece, tg.shape[4]),
                (((0,), (0,)), ((), ())), preferred_element_type=jnp.float32,
            )
            lo = 1 - d // 2
            pltpu.make_async_remote_copy(
                ob.at[c, h], out.at[pl.ds(pl.multiple_of(hi * tile + c * kc, kc), kc), :],
                o_send, o_recv,
                device_id=(h * NZ + z, y, lo * 2 + d % 2), device_id_type=MESH,
            ).start()

    groups = CHUNKS // GROUP

    for j in range(GROUP):
        scatter_basis(j)
    gather_targets_x()

    def step(g, carry):
        for hop in range(4):
            for j in range(GROUP):
                c = g * GROUP + j
                if hop == 0:
                    wait_bytes(origin(c, z), x_recv.at[c])
                for way in range(2):
                    if hop > 0:
                        z_wait(c, way, hop - 1)
                    z_copy(c, way, hop).start()
            if hop == 0:
                pl.when(g == 0)(gather_targets_y)

                @pl.when(g < groups - 1)
                def _():
                    for j in range(GROUP):
                        scatter_basis((g + 1) * GROUP + j)

            if hop == 1:
                @pl.when(g > 0)
                def _():
                    @pl.when(g == 1)
                    def _():
                        wait_bytes(tg.at[:, pl.ds(0, 6)], t_recv.at[1])

                    for j in range(GROUP):
                        c = (g - 1) * GROUP + j
                        for way in range(2):
                            z_wait(c, way, 3)
                        multiply(c)
        return carry

    lax.fori_loop(0, groups, step, 0)
    for j in range(GROUP):
        c = CHUNKS - GROUP + j
        for way in range(2):
            z_wait(c, way, 3)
        multiply(c)

    wait_bytes(gath.at[:, pl.ds(0, (NX - 1) * rows), :], x_send)
    for way in range(2):
        wait_bytes(gath.at[:, pl.ds(0, 3 * piece + half), :], z_send.at[way])
    wait_bytes(tg.at[0, pl.ds(0, 4), pl.ds(0, NX - 1)], t_send.at[0])
    wait_bytes(tg.at[:, pl.ds(0, 6)], t_send.at[1])
    wait_bytes(ob, o_send)
    wait_bytes(out, o_recv)


def per_device(basis, targets):
    rows, columns = basis.shape[1:]
    samples, outs = targets.shape[1:]
    tile = columns // NX
    kc = tile // CHUNKS
    return pl.pallas_call(
        kernel,
        out_shape=jax.ShapeDtypeStruct((2 * tile, outs), jnp.float32),
        in_specs=[pl.BlockSpec(memory_space=pl.ANY)] * 2,
        out_specs=pl.BlockSpec(memory_space=pl.ANY),
        scratch_shapes=[
            pltpu.VMEM((CHUNKS, NZ * NX * rows, kc), jnp.bfloat16),
            pltpu.VMEM((2, NZ, NX, rows, outs), jnp.bfloat16),
            pltpu.VMEM((CHUNKS, 2, kc, outs), jnp.float32),
            pltpu.SemaphoreType.DMA,
            pltpu.SemaphoreType.DMA((CHUNKS,)),
            pltpu.SemaphoreType.DMA((2,)),
            pltpu.SemaphoreType.DMA((2, CHUNKS, 4)),
            pltpu.SemaphoreType.DMA((2,)),
            pltpu.SemaphoreType.DMA((2,)),
            pltpu.SemaphoreType.DMA,
            pltpu.SemaphoreType.DMA,
        ],
        compiler_params=pltpu.CompilerParams(
            collective_id=1, has_side_effects=True, vmem_limit_bytes=48 * 2**20
        ),
        name="cross",
    )(basis.reshape(rows, columns), targets.reshape(samples // rows, rows, outs))


def solution(mesh):
    in_specs = (P("depth", "row", "col"), P("depth", "col", "row"))
    out_specs = P(("col", "depth"), "row")
    return jax.shard_map(
        per_device, mesh=mesh, in_specs=in_specs, out_specs=out_specs, check_vma=False
    )
```

time: 408 us -> 113 us (0.28)
  the two profiles are of different devices: /device:TPU:1 before, /device:TPU:32 now
where the time goes in v1:
time: 113 us; the launch traced here: 112 us
  Pallas kernels  108 us (96%)
  local copies, waits for them, and re-layouts  4.08 us (4%)
    pallas_call x1, Pallas kernels, per_device(): pl.pallas_call(kernel, out_shape=jax.ShapeDtypeStruct((2 * tile, outs), j...  108 us
    unnamed x5, local copies, waits for them, and re-layouts  4.08 us

profile of v1, /device:TPU:32, one launch (start us, length us, event | category | flops | bytes accessed | tf_op | source)
XLA Modules:
  0.0 112.4 jit_solution(12456932139121823902)
XLA Ops:
  0.0 0.0 copy-start
  0.0 1.2 %copy-done = bf16[1,32,16384]{2,1,0:T(8,128)(2,1)S(1)} copy-done((bf16[1,32,16384]{2,1,0:T(8,128)(2,1)S(1)}, bf16[1,32,16384]{2,1,0:T(8,128)(2,1)}, u32[]{:S(2)}) %copy-start) | copy-done | bytes 1048600
  1.2 0.0 copy-start.1
  1.2 0.8 copy-done.1
  2.1 108.3 %cross.1 = f32[4096,256]{1,0:T(8,128)S(1)} custom-call(bf16[32,16384]{1,0:T(8,128)(2,1)S(1)} %bitcast.2, bf16[4,32,256]{2,1,0:T(8,128)(2,1)S(1)} %bitcast.3), custom_call_target="tpu_custom_call" | custom-call | tf_op jit(solution)/shard_map/cross/pallas_call | solution.py:182
  110.4 2.0 %copy.4 = f32[4096,256]{1,0:T(8,128)} copy(f32[4096,256]{1,0:T(8,128)S(1)} %cross.1) | data formatting | bytes 8388608
Async XLA Ops:
  0.0 1.2 %copy-start = (bf16[1,32,16384]{2,1,0:T(8,128)(2,1)S(1)}, bf16[1,32,16384]{2,1,0:T(8,128)(2,1)}, u32[]{:S(2)}) copy-start(bf16[1,32,16384]{2,1,0:T(8,128)(2,1)} %param.2) | copy-start | bytes 3145732
  1.2 0.8 copy-start.1

commit v2 on v0

v2 whole, which is shorter than its diff:
```python
import jax
import jax.numpy as jnp
from jax import lax
from jax.experimental import pallas as pl
from jax.experimental.pallas import tpu as pltpu
from jax.sharding import PartitionSpec as P

MESH = pl.DeviceIdType.MESH
NZ = 8
NX = 8
CHUNKS = 16
WHEN = (0, 2, 4, 6, 8)
AHEAD = 3
PRIO_Z, PRIO_X, PRIO_O = 0, 0, 0
LOCAL = -1


def kernel(
    basis, targets, out, gath, tg, ob,
    own_sem, x_send, x_recv, z_send, z_recv, t_send, t_recv, o_send, o_recv,
):
    kc = gath.shape[2]
    tile = CHUNKS * kc
    rows = basis.shape[0]
    block = NX * rows
    row, y, d = (lax.axis_index(a) for a in ("row", "col", "depth"))
    hi, z = row // NZ, row % NZ
    lo, core = d // 2, d % 2
    up, down = (z + 1) % NZ, (z + NZ - 1) % NZ

    def flip(bit, i):
        return 1 - bit if i else bit

    def x_peer(i):
        return flip(hi, i & 4), flip(lo, i & 2), flip(core, i & 1)

    def x_device(i):
        h, l, k = x_peer(i)
        return (h * NZ + z, y, l * 2 + k)

    def z_device(way):
        return (hi * NZ + (up if way == 0 else down), y, d)

    def y_device(i):
        return (row, (y + i) % 4, d)

    def columns(i, c):
        h, l, k = x_peer(i)
        start = ((1 - l) * 2 + k) * 2 * tile + h * tile + c * kc
        return pl.ds(pl.multiple_of(start, kc), kc)

    def rows_of(zz, first, count):
        return pl.ds(pl.multiple_of(zz * block + first, 16), count)

    def wait_bytes(ref, sem):
        pltpu.make_async_copy(ref, ref, sem).wait()

    for c in range(CHUNKS):
        pltpu.make_async_copy(
            basis.at[:, columns(0, c)], gath.at[c, rows_of(z, 0, rows), :], own_sem
        ).start()

    barrier = pltpu.get_barrier_semaphore()
    friends = [x_device(i) for i in range(1, NX)] + [z_device(0), z_device(1)]
    friends += [y_device(i) for i in range(1, 4)]
    for friend in friends:
        pl.semaphore_signal(barrier, inc=1, device_id=friend, device_id_type=MESH)
    pl.semaphore_wait(barrier, len(friends))

    def scatter_basis(c):
        for i in range(1, NX):
            pltpu.make_async_remote_copy(
                basis.at[:, columns(i, c)], gath.at[c, rows_of(z, i * rows, rows), :],
                x_send, x_recv.at[c], device_id=x_device(i), device_id_type=MESH,
            ).start(priority=PRIO_X)

    def z_part(c, zz, way, hop):
        local = isinstance(c, int)
        first, count = (0, rows) if local else (rows, block - rows)
        if hop == 3:
            count //= 2
            first += way * count
        if local:
            return gath.at[:, rows_of(zz, first, count), :]
        return gath.at[c, rows_of(zz, first, count), :]

    def z_origin(way, hop):
        return (z - hop + NZ) % NZ if way == 0 else (z + hop) % NZ

    def z_send_hop(c, way, hop):
        ref = z_part(c, z_origin(way, hop), way, hop)
        pltpu.make_async_remote_copy(
            ref, ref, z_send.at[way], z_recv.at[way, c + 1, hop],
            device_id=z_device(way), device_id_type=MESH,
        ).start(priority=PRIO_Z)

    def z_wait(c, way, hop):
        wait_bytes(z_part(c, z_origin(way, hop + 1), way, hop), z_recv.at[way, c + 1, hop])

    def t_region(yy):
        half = yy // 2 + hi - 2 * (yy // 2) * hi
        return tg.at[:, pl.ds((yy % 2) * 4, 4), pl.ds(half * 4, 4), :, :]

    def t_block(i):
        h = x_peer(i)[0]
        half = y // 2 + h - 2 * (y // 2) * h
        return tg.at[hi, pl.ds((y % 2) * 4, 4), half * 4 + i % 4, :, :]

    def gather_targets_x():
        for i in range(1, NX):
            pltpu.make_async_remote_copy(
                targets, t_block(i), t_send.at[0], t_recv.at[0],
                device_id=x_device(i), device_id_type=MESH,
            ).start(priority=PRIO_X)
        pltpu.make_async_copy(targets, t_block(0), t_recv.at[0]).start()

    def gather_targets_y():
        wait_bytes(t_region(y), t_recv.at[0])
        for i in (2, 1, 3):
            pltpu.make_async_remote_copy(
                t_region(y), t_region(y), t_send.at[1], t_recv.at[1],
                device_id=y_device(i), device_id_type=MESH,
            ).start(priority=PRIO_X)

    def multiply(c):
        a = gath[c]
        for h in range(2):
            ob[c, h] = lax.dot_general(
                a, tg[h].reshape(NZ * block, tg.shape[4]),
                (((0,), (0,)), ((), ())), preferred_element_type=jnp.float32,
            )
            pltpu.make_async_remote_copy(
                ob.at[c, h], out.at[pl.ds(pl.multiple_of(hi * tile + c * kc, kc), kc), :],
                o_send, o_recv,
                device_id=(h * NZ + z, y, (1 - lo) * 2 + core), device_id_type=MESH,
            ).start(priority=PRIO_O)

    def forward(c, hop):
        for way in range(2):
            if hop:
                z_wait(c, way, hop - 1)
            z_send_hop(c, way, hop)

    wait_bytes(gath.at[:, rows_of(z, 0, rows), :], own_sem)
    forward(LOCAL, 0)
    for c in range(AHEAD):
        scatter_basis(c)
    gather_targets_x()

    def step(t, carry):
        for hop in (3, 2, 1):
            c = t - WHEN[hop]
            pl.when(c == LOCAL)(lambda: forward(LOCAL, hop))
            pl.when((c >= 0) & (c < CHUNKS))(lambda: forward(c, hop))

        @pl.when(t < CHUNKS)
        def _():
            wait_bytes(gath.at[t, rows_of(z, rows, block - rows), :], x_recv.at[t])
            forward(t, 0)

        pl.when(t == 1)(gather_targets_y)

        @pl.when(t + AHEAD < CHUNKS)
        def _():
            scatter_basis(t + AHEAD)

        c = t - WHEN[4]

        @pl.when(c == LOCAL)
        def _():
            for way in range(2):
                z_wait(LOCAL, way, 3)
            wait_bytes(tg.at[:, pl.ds(0, 6)], t_recv.at[1])

        @pl.when(c >= 0)
        def _():
            for way in range(2):
                z_wait(c, way, 3)
            multiply(c)

        return carry

    lax.fori_loop(0, CHUNKS + WHEN[4], step, 0)

    wait_bytes(gath.at[:, pl.ds(0, block - rows), :], x_send)
    for way in range(2):
        wait_bytes(gath.at[:, pl.ds(0, 3 * block + block // 2), :], z_send.at[way])
    wait_bytes(tg.at[0, pl.ds(0, 4), pl.ds(0, NX - 1)], t_send.at[0])
    wait_bytes(tg.at[:, pl.ds(0, 6)], t_send.at[1])
    wait_bytes(ob, o_send)
    wait_bytes(out, o_recv)


def per_device(basis, targets):
    rows, columns = basis.shape[1:]
    samples, outs = targets.shape[1:]
    tile = columns // NX
    kc = tile // CHUNKS
    return pl.pallas_call(
        kernel,
        out_shape=jax.ShapeDtypeStruct((2 * tile, outs), jnp.float32),
        in_specs=[pl.BlockSpec(memory_space=pl.ANY)] * 2,
        out_specs=pl.BlockSpec(memory_space=pl.ANY),
        scratch_shapes=[
            pltpu.VMEM((CHUNKS, NZ * NX * rows, kc), jnp.bfloat16),
            pltpu.VMEM((2, NZ, NX, rows, outs), jnp.bfloat16),
            pltpu.VMEM((CHUNKS, 2, kc, outs), jnp.float32),
            pltpu.SemaphoreType.DMA,
            pltpu.SemaphoreType.DMA,
            pltpu.SemaphoreType.DMA((CHUNKS,)),
            pltpu.SemaphoreType.DMA((2,)),
            pltpu.SemaphoreType.DMA((2, CHUNKS + 1, 4)),
            pltpu.SemaphoreType.DMA((2,)),
            pltpu.SemaphoreType.DMA((2,)),
            pltpu.SemaphoreType.DMA,
            pltpu.SemaphoreType.DMA,
        ],
        compiler_params=pltpu.CompilerParams(
            collective_id=1, has_side_effects=True, vmem_limit_bytes=48 * 2**20
        ),
        name="cross",
    )(
        pltpu.with_memory_space_constraint(basis.reshape(rows, columns), pltpu.HBM),
        pltpu.with_memory_space_constraint(
            targets.reshape(samples // rows, rows, outs), pltpu.HBM
        ),
    )


def solution(mesh):
    in_specs = (P("depth", "row", "col"), P("depth", "col", "row"))
    out_specs = P(("col", "depth"), "row")
    return jax.shard_map(
        per_device, mesh=mesh, in_specs=in_specs, out_specs=out_specs, check_vma=False
    )
```

time: 408 us -> 108 us (0.26)
  waiting for transfers between devices: 367 us -> 0 us
  Pallas kernels: 0 us -> 106 us
  matrix products: 16 us -> 0 us
  between operations: 13.4 us -> 0.01 us
  blocking collectives: 11.5 us -> 0 us
    all_gather x1 -> x0, waiting for transfers between devices: 220 us -> none  [per_device(): lax.all_gather(basis, 'row', axis=1, tiled=True)[0]]
    reduce_scatter x1 -> x0, waiting for transfers between devices: 147 us -> none  [per_device(): lax.psum_scatter(partial_cross, 'depth', scatter_dimension=0, tiled=True)]
    pallas_call x0 -> x1, Pallas kernels: none -> 106 us  [per_device(): pl.pallas_call(kernel, out_shape=jax.ShapeDtypeStruct((2 * tile, outs), j...]
    dot_general x1 -> x0, matrix products: 16 us -> none  [per_device(): jnp.einsum('sk,so->ko', lax.all_gather(basis, 'row', axis=1, tiled=True)[...]
    all_gather x1 -> x0, blocking collectives: 11.5 us -> none  [per_device(): layer_targets = lax.all_gather(targets, 'col', axis=1, tiled=True)]
  transfers between devices with their start and end apart: 2 -> 0, of which waited for: 2 -> 0; matrix products, arithmetic and copies ran while one was open for 0% -> 0% of each run, Pallas kernels for 0% -> 0%
where the time goes in v2:
time: 108 us
  Pallas kernels  106 us (98%)
  local copies, waits for them, and re-layouts  2.02 us (2%)
    pallas_call x1, Pallas kernels, per_device(): pl.pallas_call(kernel, out_shape=jax.ShapeDtypeStruct((2 * tile, outs), j...  106 us

profile of v2, /device:TPU:1, one launch (start us, length us, event | category | flops | bytes accessed | tf_op | source)
XLA Modules:
  0.0 107.8 jit_solution(7597661662936757255)
XLA Ops:
  0.0 105.8 %cross.1 = f32[4096,256]{1,0:T(8,128)S(1)} custom-call(bf16[32,16384]{1,0:T(8,128)(2,1)} %bitcast.2, bf16[4,32,256]{2,1,0:T(8,128)(2,1)} %bitcast.3), custom_call_target="tpu_custom_call" | custom-call | tf_op jit(solution)/shard_map/cross/pallas_call | solution.py:199
  105.8 2.0 %copy.4 = f32[4096,256]{1,0:T(8,128)} copy(f32[4096,256]{1,0:T(8,128)S(1)} %cross.1) | data formatting | bytes 8388608

commit v3 on v2

--- a/solution.py
+++ b/solution.py
@@ -11,13 +11,12 @@
 CHUNKS = 16
 WHEN = (0, 2, 4, 6, 8)
 AHEAD = 3
-PRIO_Z, PRIO_X, PRIO_O = 0, 0, 0
-LOCAL = -1
+WAVES = 2
 
 
 def kernel(
     basis, targets, out, gath, tg, ob,
-    own_sem, x_send, x_recv, z_send, z_recv, t_send, t_recv, o_send, o_recv,
+    own_sem, e_recv, x_send, x_recv, z_send, z_recv, t_send, t_recv, o_send, o_recv,
 ):
     kc = gath.shape[2]
     tile = CHUNKS * kc
@@ -68,15 +67,25 @@
     pl.semaphore_wait(barrier, len(friends))
 
     def scatter_basis(c):
-        for i in range(1, NX):
+        for i in range(WAVES, NX):
             pltpu.make_async_remote_copy(
                 basis.at[:, columns(i, c)], gath.at[c, rows_of(z, i * rows, rows), :],
                 x_send, x_recv.at[c], device_id=x_device(i), device_id_type=MESH,
-            ).start(priority=PRIO_X)
+            ).start()
+
+    def scatter_early():
+        for i in range(1, WAVES):
+            for c in range(CHUNKS):
+                pltpu.make_async_remote_copy(
+                    basis.at[:, columns(i, c)], gath.at[c, rows_of(z, i * rows, rows), :],
+                    x_send, e_recv.at[i], device_id=x_device(i), device_id_type=MESH,
+                ).start()
 
     def z_part(c, zz, way, hop):
         local = isinstance(c, int)
-        first, count = (0, rows) if local else (rows, block - rows)
+        first, count = WAVES * rows, block - WAVES * rows
+        if local:
+            first, count = (c + WAVES) * rows, rows
         if hop == 3:
             count //= 2
             first += way * count
@@ -90,12 +99,12 @@
     def z_send_hop(c, way, hop):
         ref = z_part(c, z_origin(way, hop), way, hop)
         pltpu.make_async_remote_copy(
-            ref, ref, z_send.at[way], z_recv.at[way, c + 1, hop],
+            ref, ref, z_send.at[way], z_recv.at[way, c + WAVES, hop],
             device_id=z_device(way), device_id_type=MESH,
-        ).start(priority=PRIO_Z)
+        ).start()
 
     def z_wait(c, way, hop):
-        wait_bytes(z_part(c, z_origin(way, hop + 1), way, hop), z_recv.at[way, c + 1, hop])
+        wait_bytes(z_part(c, z_origin(way, hop + 1), way, hop), z_recv.at[way, c + WAVES, hop])
 
     def t_region(yy):
         half = yy // 2 + hi - 2 * (yy // 2) * hi
@@ -111,7 +120,7 @@
             pltpu.make_async_remote_copy(
                 targets, t_block(i), t_send.at[0], t_recv.at[0],
                 device_id=x_device(i), device_id_type=MESH,
-            ).start(priority=PRIO_X)
+            ).start()
         pltpu.make_async_copy(targets, t_block(0), t_recv.at[0]).start()
 
     def gather_targets_y():
@@ -120,7 +129,7 @@
             pltpu.make_async_remote_copy(
                 t_region(y), t_region(y), t_send.at[1], t_recv.at[1],
                 device_id=y_device(i), device_id_type=MESH,
-            ).start(priority=PRIO_X)
+            ).start()
 
     def multiply(c):
         a = gath[c]
@@ -133,7 +142,7 @@
                 ob.at[c, h], out.at[pl.ds(pl.multiple_of(hi * tile + c * kc, kc), kc), :],
                 o_send, o_recv,
                 device_id=(h * NZ + z, y, (1 - lo) * 2 + core), device_id_type=MESH,
-            ).start(priority=PRIO_O)
+            ).start()
 
     def forward(c, hop):
         for way in range(2):
@@ -142,22 +151,27 @@
             z_send_hop(c, way, hop)
 
     wait_bytes(gath.at[:, rows_of(z, 0, rows), :], own_sem)
-    forward(LOCAL, 0)
+    forward(-WAVES, 0)
+    scatter_early()
     for c in range(AHEAD):
         scatter_basis(c)
+    for i in range(1, WAVES):
+        wait_bytes(gath.at[:, rows_of(z, i * rows, rows), :], e_recv.at[i])
+        forward(i - WAVES, 0)
     gather_targets_x()
 
     def step(t, carry):
-        for hop in (3, 2, 1):
+        @pl.when(t < CHUNKS)
+        def _():
+            wait_bytes(gath.at[t, rows_of(z, WAVES * rows, block - WAVES * rows), :], x_recv.at[t])
+            forward(t, 0)
+
+        for hop in (1, 2, 3):
             c = t - WHEN[hop]
-            pl.when(c == LOCAL)(lambda: forward(LOCAL, hop))
+            for wave in range(-WAVES, 0):
+                pl.when(c == wave)(lambda: forward(wave, hop))
             pl.when((c >= 0) & (c < CHUNKS))(lambda: forward(c, hop))
 
-        @pl.when(t < CHUNKS)
-        def _():
-            wait_bytes(gath.at[t, rows_of(z, rows, block - rows), :], x_recv.at[t])
-            forward(t, 0)
-
         pl.when(t == 1)(gather_targets_y)
 
         @pl.when(t + AHEAD < CHUNKS)
@@ -166,10 +180,11 @@
 
         c = t - WHEN[4]
 
-        @pl.when(c == LOCAL)
+        @pl.when(c == -1)
         def _():
             for way in range(2):
-                z_wait(LOCAL, way, 3)
+                for wave in range(-WAVES, 0):
+                    z_wait(wave, way, 3)
             wait_bytes(tg.at[:, pl.ds(0, 6)], t_recv.at[1])
 
         @pl.when(c >= 0)
@@ -206,10 +221,11 @@
             pltpu.VMEM((2, NZ, NX, rows, outs), jnp.bfloat16),
             pltpu.VMEM((CHUNKS, 2, kc, outs), jnp.float32),
             pltpu.SemaphoreType.DMA,
+            pltpu.SemaphoreType.DMA((WAVES,)),
             pltpu.SemaphoreType.DMA,
             pltpu.SemaphoreType.DMA((CHUNKS,)),
             pltpu.SemaphoreType.DMA((2,)),
-            pltpu.SemaphoreType.DMA((2, CHUNKS + 1, 4)),
+            pltpu.SemaphoreType.DMA((2, CHUNKS + WAVES, 4)),
             pltpu.SemaphoreType.DMA((2,)),
             pltpu.SemaphoreType.DMA((2,)),
             pltpu.SemaphoreType.DMA,

time: 108 us -> 106 us (0.981)
  Pallas kernels: 106 us -> 104 us
    pallas_call x1, Pallas kernels: 106 us -> 104 us  [per_device(): pl.pallas_call(kernel, out_shape=jax.ShapeDtypeStruct((2 * tile, outs), j...]
where the time goes in v3:
time: 106 us
  Pallas kernels  104 us (98%)
  local copies, waits for them, and re-layouts  2.02 us (2%)
    pallas_call x1, Pallas kernels, per_device(): pl.pallas_call(kernel, out_shape=jax.ShapeDtypeStruct((2 * tile, outs), j...  104 us

profile of v3, /device:TPU:1, one launch (start us, length us, event | category | flops | bytes accessed | tf_op | source)
XLA Modules:
  0.0 105.8 jit_solution(16169951809949010650)
XLA Ops:
  0.0 103.7 %cross.1 = f32[4096,256]{1,0:T(8,128)S(1)} custom-call(bf16[32,16384]{1,0:T(8,128)(2,1)} %bitcast.2, bf16[4,32,256]{2,1,0:T(8,128)(2,1)} %bitcast.3), custom_call_target="tpu_custom_call" | custom-call | tf_op jit(solution)/shard_map/cross/pallas_call | solution.py:214
  103.8 2.0 %copy.4 = f32[4096,256]{1,0:T(8,128)} copy(f32[4096,256]{1,0:T(8,128)S(1)} %cross.1) | data formatting | bytes 8388608

commit v4 on v3

--- a/solution.py
+++ b/solution.py
@@ -10,6 +10,7 @@
 NX = 8
 CHUNKS = 16
 WHEN = (0, 2, 4, 6, 8)
+TAIL = CHUNKS + 1
 AHEAD = 3
 WAVES = 2
 
@@ -160,7 +161,14 @@
         forward(i - WAVES, 0)
     gather_targets_x()
 
+    def finish(c):
+        for way in range(2):
+            z_wait(c, way, 3)
+        multiply(c)
+
     def step(t, carry):
+        pl.when(t >= TAIL)(lambda: finish(t - WHEN[4]))
+
         @pl.when(t < CHUNKS)
         def _():
             wait_bytes(gath.at[t, rows_of(z, WAVES * rows, block - WAVES * rows), :], x_recv.at[t])
@@ -187,11 +195,9 @@
                     z_wait(wave, way, 3)
             wait_bytes(tg.at[:, pl.ds(0, 6)], t_recv.at[1])
 
-        @pl.when(c >= 0)
-        def _():
-            for way in range(2):
-                z_wait(c, way, 3)
-            multiply(c)
+        @pl.when((c >= 0) & (t < TAIL))
+        def _():
+            finish(c)
 
         return carry
 

time: 106 us -> 106 us (level)
  no operation moved by 1% of the time
where the time goes in v4:
time: 106 us
  Pallas kernels  104 us (98%)
  local copies, waits for them, and re-layouts  2.02 us (2%)
    pallas_call x1, Pallas kernels, per_device(): pl.pallas_call(kernel, out_shape=jax.ShapeDtypeStruct((2 * tile, outs), j...  104 us

profile of v4, /device:TPU:1, one launch (start us, length us, event | category | flops | bytes accessed | tf_op | source)
XLA Modules:
  0.0 106.0 jit_solution(17632965223476896199)
XLA Ops:
  0.0 103.9 %cross.1 = f32[4096,256]{1,0:T(8,128)S(1)} custom-call(bf16[32,16384]{1,0:T(8,128)(2,1)} %bitcast.2, bf16[4,32,256]{2,1,0:T(8,128)(2,1)} %bitcast.3), custom_call_target="tpu_custom_call" | custom-call | tf_op jit(solution)/shard_map/cross/pallas_call | solution.py:220
  103.9 2.0 %copy.4 = f32[4096,256]{1,0:T(8,128)} copy(f32[4096,256]{1,0:T(8,128)S(1)} %cross.1) | data formatting | bytes 8388608
